TPU v7x, 32 devices: a whole 2x2x4 slice. The times are simulated.
32 devices in a mesh: band: 4 (over x, core), inp: 8 (over z, y).
Axes of the slice: x: 2, y: 2, z: 4, core: 2. Of those that a mesh axis runs over, the one named last changes fastest.
Arguments:
- spectra: float32 [1024, 512, 256], P('inp', 'band'), parts along dimension 1, may hold values from -6 to 6
- delays: int32 [1024], replicated, may hold values from 0 to 127
- owner_bounds: int32 [9], replicated, may hold values from 0 to 4608, as said below
Outputs:
- owned: float32 [128, 7680, 256], P('band', 'inp'), parts along dimension 0
There are 4 independent parts, one for each index of `band`. A program takes and returns all parts, laid end to end along the dimension named above; an argument that names none is the same for every part. Nothing has to cross between parts.
Inputs may be any that keep to these rules, and one draw needn't show every extreme that they name: owner_bounds[0] = 0, owner_bounds[8] = 4608, rising; each owner_bounds[k] lies within 192 of k * 576; every owner holds at most 960 rows and some owner exactly 960.
All inputs are finite; a program needn't handle non-finite values.
Results may differ from a plain program's by a relative error of at most 0.000086.
Values sent between devices are 32-bit elements; how exact they have to be, the bound alone decides.
A program may use at most 256 MiB of HBM per device.

v0:
```python
import math

import jax
import jax.numpy as jnp
from jax import lax
from jax.sharding import PartitionSpec as P

CH = 128
AVG = 4
TILE = 128


def cross_product(left_side, right_side):
    return lax.dot_general(
        left_side,
        right_side,
        (((1,), (1,)), ((), ())),
        precision=lax.Precision.HIGHEST,
        preferred_element_type=jnp.float32,
    )


def pack_tile_rows(real_rows, imag_rows, row_tile):
    pieces = []
    for col_tile in range(row_tile + 1):
        pieces.append(
            jnp.concatenate(
                [
                    real_rows[:, col_tile * TILE : (col_tile + 1) * TILE],
                    imag_rows[:, col_tile * TILE : (col_tile + 1) * TILE],
                ],
                axis=1,
            )
        )
    return jnp.concatenate(pieces, axis=0)


def correct(turned, delays, first_chan):
    inputs, local_chans, row_len = turned.shape
    samples = row_len // 2
    channel = first_chan + jnp.arange(local_chans, dtype=jnp.int32)
    phase_steps = delays[:, None] * channel[None, :] % CH
    phase_angle = (phase_steps.astype(jnp.float32) * (2.0 * math.pi / CH))[:, :, None]
    cos_part = jnp.cos(phase_angle)
    sine_part = jnp.sin(phase_angle)
    real_part = turned[:, :, :samples]
    imag_part = turned[:, :, samples:]
    fixed_re = real_part * cos_part + imag_part * sine_part
    fixed_im = imag_part * cos_part - real_part * sine_part
    local_vis = local_chans // AVG
    direct = jnp.concatenate([fixed_re, fixed_im], axis=2).reshape(inputs, local_vis, AVG * row_len)
    swapped = jnp.concatenate([fixed_im, -fixed_re], axis=2).reshape(
        inputs, local_vis, AVG * row_len
    )
    return (direct, swapped)


def per_device(spectra, delays, owner_bounds):
    n_devices = lax.axis_size("inp")
    my_index = lax.axis_index("inp")
    turned = lax.all_to_all(spectra, "inp", split_axis=1, concat_axis=0, tiled=True)
    inputs, local_chans, row_len = turned.shape
    samples = row_len // 2
    norm_scale = 1.0 / (AVG * samples)
    direct, swapped = correct(turned, delays, my_index * local_chans)
    local_vis = local_chans // AVG
    tile_count = inputs // TILE
    packed_list = []
    for vis_index in range(local_vis):
        left_all = direct[:, vis_index]
        swap_all = swapped[:, vis_index]
        pieces = []
        square_re = cross_product(left_all, left_all) * norm_scale
        square_im = cross_product(swap_all, left_all) * norm_scale
        for row_tile in range(tile_count):
            pieces.append(
                pack_tile_rows(
                    square_re[row_tile * TILE : (row_tile + 1) * TILE],
                    square_im[row_tile * TILE : (row_tile + 1) * TILE],
                    row_tile,
                )
            )
        packed_list.append(jnp.concatenate(pieces, axis=0))
    packed = jnp.stack(packed_list, axis=0)
    rows_total = packed.shape[1]
    block_rows = rows_total // n_devices
    margin_rows = block_rows // 3
    slot_rows = block_rows + 2 * margin_rows
    slot_ids = jnp.arange(slot_rows, dtype=jnp.int32)
    counts = owner_bounds[1:] - owner_bounds[:-1]
    is_live = slot_ids[None, :] < counts[:, None]
    row_index = jnp.where(is_live, owner_bounds[:-1, None] + slot_ids[None, :], 0).reshape(-1)
    picked = jnp.take(packed, row_index, axis=1)
    outgoing = jnp.where(is_live.reshape(-1)[None, :, None], picked, jnp.zeros_like(picked))
    result = lax.all_to_all(outgoing, "inp", split_axis=1, concat_axis=0, tiled=True)
    return result


def solution(mesh):
    placed = (P("inp", "band", None), P(), P())
    return jax.shard_map(
        per_device, mesh=mesh, in_specs=placed, out_specs=P("band", "inp", None), check_vma=False
    )
```

profile of v0, /device:TPU:24, one launch (start us, length us, event | category | flops | bytes accessed | tf_op | source)
XLA Modules:
  0.0 1483.7 jit_solution(15595072913385701790)
XLA Ops:
  0.0 17.8 %copy.17 = f32[128,128,256]{2,0,1:T(8,128)} copy(f32[128,128,256]{2,1,0:T(8,128)} %param.3) | data formatting | bytes 33554432 | tf_op args[0]
  17.8 6.4 all-to-all-start
  26.8 358.8 %all-to-all-done = f32[128,128,256]{2,0,1:T(8,128)} async-done(((f32[128,128,256]{2,0,1:T(8,128)}), f32[128,128,256]{2,0,1:T(8,128)}, u32[]{:S(2)}, u32[]{:S(2)}) %all-to-all-start) | async-done | bytes 16777248 | tf_op jit(solution)/shard_map/all_to_all | solution.py:61
  385.6 15.2 %copy.19 = f32[8,128,16,256]{3,2,1,0:T(8,128)S(1)} copy(f32[8,128,16,256]{3,1,2,0:T(8,128)} %bitcast.2) | data formatting | bytes 33554432 | tf_op jit(solution)/shard_map/all_to_all | solution.py:61
  400.9 8.2 fusion.70
  409.0 17.4 %pad_maximum_fusion.2 = (f32[1024,16,256]{2,1,0:T(8,128)}, f32[1024,16,256]{2,1,0:T(8,128)}) fusion(f32[1024,16,128]{2,1,0:T(8,128)S(1)} %get-tuple-element.5, f32[1024,16,128]{2,1,0:T(8,128)} %get-tuple-element.7, f32[1024,16,128]{2,1,0:T(8,128)S(1)} %get-tuple-element.6), kind=kLoop, calls=%fused_computation.4 | loop fusion | flops 8388608 | bytes 58720256 | tf_op jit(solution)/shard_map/concatenate | solution.py:52
  426.5 20.4 %reshape.164 = f32[1024,4,1024]{2,1,0:T(4,128)} reshape(f32[1024,16,256]{2,1,0:T(8,128)} %get-tuple-element.17) | data formatting | bytes 33554432 | tf_op jit(solution)/shard_map/reshape | solution.py:51
  446.8 20.4 %reshape.165 = f32[1024,4,1024]{2,1,0:T(4,128)} reshape(f32[1024,16,256]{2,1,0:T(8,128)} %get-tuple-element.16) | data formatting | bytes 33554432 | tf_op jit(solution)/shard_map/reshape | solution.py:52
  467.2 70.8 %fusion.71 = (f32[1024,1,1024]{2,1,0:T(1,128)}, f32[1024,1,1024]{2,1,0:T(1,128)S(1)}, f32[1024,1,1024]{2,1,0:T(1,128)}, f32[1024,1,1024]{2,1,0:T(1,128)}, f32[10...) fusion(f32[1024,4,1024]{2,1,0:T(4,128)} %reshape.165, ...), kind=kLoop, calls=%fused_computation.212 | loop fusion | bytes 67108864 | tf_op jit(solution)/shard_map/slice | solution.py:71
  538.0 18.9 %fusion.32 = f32[1024,1024]{0,1:T(8,128)S(1)} fusion(f32[1024,1,1024]{2,1,0:T(1,128)} %get-tuple-element.315), kind=kOutput, calls=%fused_computation.39 | convolution fusion | flops 12885950464 | bytes 8388608 | tf_op jit(solution)/shard_map/dot_general | solution.py:14
  557.0 14.3 fusion.44
  571.3 1.0 fusion.76
  572.4 1.1 fusion.75
  573.5 0.8 fusion.73
  574.3 14.3 fusion.35
  588.6 14.5 fusion.49
  603.1 0.7 fusion.80
  604.0 0.8 fusion.79
  605.8 14.3 fusion.38
  620.1 14.4 fusion.54
  634.6 0.8 fusion.84
  635.5 0.7 fusion.83
  636.3 14.5 fusion.41
  650.8 14.7 fusion.59
  666.6 0.9 constant_dynamic-update-slice_fusion.107
  670.8 6.9 pad_maximum_fusion
  677.7 21.5 %copy.22 = f32[4,4608,256]{2,0,1:T(4,128)} copy(f32[4,4608,256]{1,2,0:T(8,128)} %pad_maximum_fusion) | data formatting | bytes 37748736 | tf_op jit(solution)/shard_map/stack | solution.py:84
  699.3 36.3 %gather_fusion = f32[7680,4,256]{2,1,0:T(4,128)} fusion(f32[4,4608,256]{2,0,1:T(4,128)} %copy.22, s32[8192]{0:T(1024)S(1)} %copy-done.50), kind=kCustom, calls=%fused_computation | custom fusion | bytes 62945280 | tf_op jit(solution)/shard_map/jit(_take)/gather | solution.py:93
  735.6 40.9 %select_bitcast_fusion = f32[4,7680,256]{2,0,1:T(4,128)S(1)} fusion(f32[7680,4,256]{2,1,0:T(4,128)} %gather_fusion, pred[7680]{0:T(1024)(128)(4,1)S(1)} %copy-done.52, pred[7680]{0:T(1024)(128)(4,1)S(1)} %copy-done.53), kind=kLoop, calls=%fused_computation.1 | loop fusion | flops 15728640 | bytes 62929920 | tf_op jit(solution)/shard_map/jit(_where)/select_n | solution.py:94
  776.5 679.9 %all_to_all.36 = f32[4,7680,256]{2,0,1:T(4,128)} all-to-all(f32[4,7680,256]{2,0,1:T(4,128)S(1)} %select_bitcast_fusion), channel_id=1, replica_groups=mesh['band'=4,'inp'=8] {'inp'}, dimensions={1} | all-to-all | bytes 62914560 | tf_op jit(solution)/shard_map/all_to_all | solution.py:95
  1456.4 16.4 %copy.23 = f32[4,7680,256]{2,1,0:T(8,128)S(1)} copy(f32[4,7680,256]{2,0,1:T(4,128)} %all_to_all.36) | data formatting | bytes 62914560 | tf_op jit(solution)/shard_map/all_to_all | solution.py:95
  1472.9 10.7 copy.24
  (277 shorter events, 6.3 us)
Async XLA Ops:
  17.8 6.4 copy-start.54
  17.8 7.2 copy-start.55
  17.8 367.8 %all-to-all-start = ((f32[128,128,256]{2,0,1:T(8,128)}), f32[128,128,256]{2,0,1:T(8,128)}, u32[]{:S(2)}, u32[]{:S(2)}) async-start(f32[128,128,256]{2,0,1:T(8,128)} %copy.17), calls=%async_computation | async-start | bytes 33554432 | tf_op jit(solution)/shard_map/all_to_all | solution.py:61
  25.5 375.3 %copy-start.51 = (pred[7680]{0:T(1024)(128)(4,1)}, pred[7680]{0:T(1024)(128)(4,1)S(1)}, u32[]{:S(2)}) copy-start(pred[7680]{0:T(1024)(128)(4,1)S(1)} %lt.59) | copy-start | bytes 23044
  538.0 19.0 %copy-start.4 = (f32[1024,1,1024]{2,1,0:T(1,128)S(1)}, f32[1024,1,1024]{2,1,0:T(1,128)}, u32[]{:S(2)}) copy-start(f32[1024,1,1024]{2,1,0:T(1,128)} %get-tuple-element.8) | copy-start | bytes 12582916
  538.0 19.0 %copy-start.5 = (f32[1024,1,1024]{2,1,0:T(1,128)S(1)}, f32[1024,1,1024]{2,1,0:T(1,128)}, u32[]{:S(2)}) copy-start(f32[1024,1,1024]{2,1,0:T(1,128)} %get-tuple-element.315) | copy-start | bytes 12582916
  571.3 3.0 copy-start.3
  574.3 14.3 copy-start.2
  603.1 2.3 copy-start.1
  605.8 14.3 copy-start
  665.8 2.1 copy-start.22
  665.8 2.1 copy-start.41
  665.8 2.1 copy-start.20
  665.8 2.1 copy-start.40
  665.8 2.1 copy-start.18
  665.8 2.1 copy-start.39
  665.9 2.1 copy-start.15
  665.9 2.1 copy-start.38
  665.9 2.2 copy-start.12
  665.9 2.2 copy-start.37
  666.1 2.1 copy-start.31
  666.1 2.1 copy-start.29
  666.1 2.1 copy-start.27
  666.1 2.1 copy-start.25
  666.1 2.2 copy-start.23
  666.3 2.1 copy-start.17
  666.3 2.1 copy-start.14
  666.3 2.1 copy-start.11
  666.3 2.2 copy-start.8
  677.7 21.5 %copy-start.50 = (s32[8192]{0:T(1024)S(1)}, s32[8192]{0:T(1024)}, u32[]{:S(2)}) copy-start(s32[8192]{0:T(1024)} %pad_clamp_fusion) | copy-start | bytes 98308
  699.3 36.3 %copy-start.52 = (pred[7680]{0:T(1024)(128)(4,1)S(1)}, pred[7680]{0:T(1024)(128)(4,1)}, u32[]{:S(2)}) copy-start(pred[7680]{0:T(1024)(128)(4,1)} %copy-done.51) | copy-start | bytes 23044
  699.3 36.3 %copy-start.53 = (pred[7680]{0:T(1024)(128)(4,1)S(1)}, pred[7680]{0:T(1024)(128)(4,1)}, u32[]{:S(2)}) copy-start(pred[7680]{0:T(1024)(128)(4,1)} %compare_and_fusion) | copy-start | bytes 23044
  (25 other events, 42.1 us)
where the time goes:
time: 1500 us; the launch traced here: 1480 us
  blocking collectives  680 us (45%)
  waiting for transfers between devices  359 us (24%)
  local copies, waits for them, and re-layouts  238 us (16%)
  matrix products  120 us (8%)
  other arithmetic  78 us (5%)
    all_to_all x1, blocking collectives, per_device(): lax.all_to_all(outgoing, 'inp', split_axis=1, concat_axis=0, tiled=True)  680 us
    all_to_all x1, waiting for transfers between devices, per_device(): lax.all_to_all(spectra, 'inp', split_axis=1, concat_axis=0, tiled=True)  359 us
    dot_general x8, matrix products, cross_product(): lax.dot_general(left_side, right_side, (((1,), (1,)), ((), ())), precisio...  120 us
    slice x1, local copies, waits for them, and re-layouts, per_device(): swap_all = swapped[:, vis_index]  70.8 us
    select_n x1, other arithmetic, per_device(): jnp.where(is_live.reshape(-1)[None, :, None], picked, jnp.zeros_like(pick...  40.9 us
    gather x1, local copies, waits for them, and re-layouts, per_device(): picked = jnp.take(packed, row_index, axis=1)  36.3 us
  transfers between devices with their start and end apart: 1, of which 1 were waited for; matrix products, arithmetic and copies ran while one was open for 0% of the time, Pallas kernels for 0%

commit v1 on v0

v1 whole, which is shorter than its diff:
```python
import functools
import math

import jax
import jax.numpy as jnp
from jax import lax
from jax.experimental import pallas as pl
from jax.experimental.pallas import tpu as pltpu
from jax.sharding import PartitionSpec as P

CH = 128
AVG = 4
TILE = 128
GROUP = 2
MESH = pl.DeviceIdType.MESH


def correlate_kernel(
    n,
    group,
    block,
    spectra_ref,
    cos_ref,
    sin_ref,
    window_ref,
    turned,
    high,
    low,
    packed,
    x_send,
    x_recv,
    mid_send,
    low_send,
    high_send,
    mid_recv,
    low_recv,
    high_recv,
    up_send,
    down_send,
):
    me = lax.axis_index("inp")
    chunks, _, sig, cc, samples = turned.shape
    row_len = 2 * samples
    inputs = spectra_ref.shape[0]
    local_vis = packed.shape[0]
    per_chunk = local_vis // chunks
    tiles = sig // TILE
    margin = block // 3
    norm = 1.0 / (AVG * samples)

    barrier = pltpu.get_barrier_semaphore()

    def greet(d, carry):
        pl.semaphore_signal(
            barrier, inc=1, device_id={"inp": lax.rem(me + d, n)}, device_id_type=MESH
        )
        return carry

    lax.fori_loop(1, n, greet, 0)
    pl.semaphore_wait(barrier, n - 1)

    def spectra_part(chunk, half, owner, source):
        return (
            spectra_ref.at[:, owner * chunks + chunk, :, pl.ds(half * samples, samples)],
            turned.at[chunk, half, pl.ds(pl.multiple_of(source * inputs, inputs), inputs)],
        )

    def spectra_to(chunk, half, target):
        src, dst = spectra_part(chunk, half, target, me)
        return pltpu.make_async_remote_copy(
            src_ref=src,
            dst_ref=dst,
            send_sem=x_send.at[chunk, half, target],
            recv_sem=x_recv.at[chunk, half, me],
            device_id={"inp": target},
            device_id_type=MESH,
        )

    def spectra_from(chunk, half, source):
        src, dst = spectra_part(chunk, half, me, source)
        return pltpu.make_async_remote_copy(
            src_ref=src,
            dst_ref=dst,
            send_sem=x_send.at[chunk, half, source],
            recv_sem=x_recv.at[chunk, half, source],
            device_id={"inp": source},
            device_id_type=MESH,
        )

    def spectra_own(chunk, half):
        src, dst = spectra_part(chunk, half, me, me)
        return pltpu.make_async_copy(src, dst, x_recv.at[chunk, half, me])

    def start_chunk(chunk, carry):
        def start_one(d, inner):
            for half in range(2):
                spectra_to(chunk, half, lax.rem(me + d, n)).start()
            return inner

        lax.fori_loop(1, n, start_one, 0)
        for half in range(2):
            spectra_own(chunk, half).start()
        return carry

    lax.fori_loop(0, chunks, start_chunk, 0)

    pieces = (
        (margin, block, mid_send, mid_recv),
        (0, margin, low_send, low_recv),
        (margin + block, margin, high_send, high_recv),
    )

    def has_piece(index, target):
        if index == 1:
            return (target % group == 0) & (target > 0)
        if index == 2:
            return (target % group == group - 1) & (target < n - 1)
        return None

    def guarded(condition, body):
        if condition is None:
            body()
        else:
            pl.when(condition)(body)

    def remote_piece(vis, target, index):
        offset, rows, send, recv = pieces[index]
        first = target * block - margin + offset
        return pltpu.make_async_remote_copy(
            src_ref=packed.at[vis, pl.ds(pl.multiple_of(first, 8), rows)],
            dst_ref=window_ref.at[me * local_vis + vis, pl.ds(offset, rows)],
            send_sem=send.at[vis, target],
            recv_sem=recv.at[vis, me],
            device_id={"inp": target},
            device_id_type=MESH,
        )

    def arrived_piece(vis, source, index):
        offset, rows, send, recv = pieces[index]
        return pltpu.make_async_remote_copy(
            src_ref=packed.at[vis, pl.ds(0, rows)],
            dst_ref=window_ref.at[source * local_vis + vis, pl.ds(offset, rows)],
            send_sem=send.at[vis, source],
            recv_sem=recv.at[vis, source],
            device_id={"inp": lax.rem(me + 1, n)},
            device_id_type=MESH,
        )

    def own_piece(vis, index):
        offset, rows, send, recv = pieces[index]
        first = me * block - margin + offset
        return pltpu.make_async_copy(
            packed.at[vis, pl.ds(pl.multiple_of(first, 8), rows)],
            window_ref.at[me * local_vis + vis, pl.ds(offset, rows)],
            recv.at[vis, me],
        )

    def stage(vis, chunk, inner_vis):
        def stage_tile(p, carry):
            for c in range(AVG):
                first = inner_vis * AVG + c
                rows = pl.ds(pl.multiple_of(p * TILE, TILE), TILE)
                picked = pl.ds(p * TILE * cc + first, TILE, stride=cc)
                real = turned.at[chunk, 0].reshape(sig * cc, samples)[picked, :]
                imag = turned.at[chunk, 1].reshape(sig * cc, samples)[picked, :]
                cosine = cos_ref[vis, rows, c : c + 1]
                sine = sin_ref[vis, rows, c : c + 1]
                fixed_re = real * cosine + imag * sine
                fixed_im = imag * cosine - real * sine
                re_high = fixed_re.astype(jnp.bfloat16)
                im_high = fixed_im.astype(jnp.bfloat16)
                re_low = (fixed_re - re_high.astype(jnp.float32)).astype(jnp.bfloat16)
                im_low = (fixed_im - im_high.astype(jnp.float32)).astype(jnp.bfloat16)
                left = pl.ds(c * row_len, samples)
                right = pl.ds(c * row_len + samples, samples)
                for store, re_part, im_part in ((high, re_high, im_high), (low, re_low, im_low)):
                    store[p, 0:TILE, left] = re_part
                    store[p, 0:TILE, right] = im_part
                    store[p, TILE : 2 * TILE, left] = -im_part
                    store[p, TILE : 2 * TILE, right] = re_part
            return carry

        lax.fori_loop(0, tiles, stage_tile, 0)

    def multiply(vis):
        depth = AVG * row_len

        def product(a, b):
            return lax.dot_general(
                a, b, (((1,), (1,)), ((), ())), preferred_element_type=jnp.float32
            )

        def row_pair(pair, carry):
            def column(q, inner):
                both = pl.ds(2 * pair, 2)
                a_high = high[both, 0:TILE, :].reshape(2 * TILE, depth)
                a_low = low[both, 0:TILE, :].reshape(2 * TILE, depth)
                b_high = high[q]
                b_low = low[q]
                total = product(a_high, b_high)
                total += product(a_high, b_low)
                total += product(a_low, b_high)
                total *= norm
                p = 2 * pair

                @pl.when(q <= p)
                def _():
                    t = p * (p + 1) // 2 + q
                    packed[vis, pl.ds(pl.multiple_of(t * TILE, TILE), TILE), :] = total[:TILE]

                t = (p + 1) * (p + 2) // 2 + q
                packed[vis, pl.ds(pl.multiple_of(t * TILE, TILE), TILE), :] = total[TILE:]
                return inner

            lax.fori_loop(0, 2 * pair + 2, column, 0)
            return carry

        lax.fori_loop(0, tiles // 2, row_pair, 0)

    def start_rows(vis):
        def start_one(d, carry):
            target = lax.rem(me + d, n)
            for index in range(3):
                guarded(
                    has_piece(index, target),
                    lambda index=index: remote_piece(vis, target, index).start(),
                )
            return carry

        lax.fori_loop(1, n, start_one, 0)
        for index in range(3):
            guarded(has_piece(index, me), lambda index=index: own_piece(vis, index).start())

    def run_chunk(chunk, carry):
        def arrived(d, inner):
            for half in range(2):
                spectra_from(chunk, half, lax.rem(me + n - d, n)).wait_recv()
            return inner

        lax.fori_loop(1, n, arrived, 0)
        for half in range(2):
            spectra_own(chunk, half).wait()

        def run_vis(inner_vis, inner):
            vis = chunk * per_chunk + inner_vis
            stage(vis, chunk, inner_vis)
            multiply(vis)
            start_rows(vis)
            return inner

        lax.fori_loop(0, per_chunk, run_vis, 0)
        return carry

    lax.fori_loop(0, chunks, run_chunk, 0)

    def relay_up(vis, source):
        row = source * local_vis + vis
        return pltpu.make_async_remote_copy(
            src_ref=window_ref.at[row, pl.ds(block, margin)],
            dst_ref=window_ref.at[row, pl.ds(0, margin)],
            send_sem=up_send.at[vis, source],
            recv_sem=low_recv.at[vis, source],
            device_id={"inp": lax.rem(me + 1, n)},
            device_id_type=MESH,
        )

    def relay_down(vis, source):
        row = source * local_vis + vis
        return pltpu.make_async_remote_copy(
            src_ref=window_ref.at[row, pl.ds(margin, margin)],
            dst_ref=window_ref.at[row, pl.ds(margin + block, margin)],
            send_sem=down_send.at[vis, source],
            recv_sem=high_recv.at[vis, source],
            device_id={"inp": lax.rem(me + n - 1, n)},
            device_id_type=MESH,
        )

    goes_up = me % group != group - 1
    goes_down = me % group != 0

    def relay_vis(vis, carry):
        def relay_source(d, inner):
            source = lax.rem(me + n - d, n)

            @pl.when(d == 0)
            def _():
                own_piece(vis, 0).wait()

            @pl.when(d > 0)
            def _():
                arrived_piece(vis, source, 0).wait_recv()

            if group > 1:

                @pl.when(goes_up)
                def _():
                    relay_up(vis, source).start()

                @pl.when(goes_down)
                def _():
                    relay_down(vis, source).start()

            return inner

        lax.fori_loop(0, n, relay_source, 0)
        return carry

    lax.fori_loop(0, local_vis, relay_vis, 0)

    def finish_vis(vis, carry):
        def finish_one(d, inner):
            other = lax.rem(me + d, n)
            for index in range(3):
                guarded(
                    has_piece(index, other),
                    lambda index=index: remote_piece(vis, other, index).wait_send(),
                )

            @pl.when(me > 0)
            def _():
                arrived_piece(vis, other, 1).wait_recv()

            @pl.when(me < n - 1)
            def _():
                arrived_piece(vis, other, 2).wait_recv()

            return inner

        lax.fori_loop(1, n, finish_one, 0)

        @pl.when(has_piece(1, me))
        def _():
            own_piece(vis, 1).wait()

        @pl.when((me > 0) & jnp.logical_not(has_piece(1, me)))
        def _():
            arrived_piece(vis, me, 1).wait_recv()

        @pl.when(has_piece(2, me))
        def _():
            own_piece(vis, 2).wait()

        @pl.when((me < n - 1) & jnp.logical_not(has_piece(2, me)))
        def _():
            arrived_piece(vis, me, 2).wait_recv()

        if group > 1:

            def finish_relay(source, inner):
                @pl.when(goes_up)
                def _():
                    relay_up(vis, source).wait_send()

                @pl.when(goes_down)
                def _():
                    relay_down(vis, source).wait_send()

                return inner

            lax.fori_loop(0, n, finish_relay, 0)
        return carry

    lax.fori_loop(0, local_vis, finish_vis, 0)

    def finish_chunk(chunk, carry):
        def finish_spectra(d, inner):
            for half in range(2):
                spectra_to(chunk, half, lax.rem(me + d, n)).wait_send()
            return inner

        lax.fori_loop(1, n, finish_spectra, 0)
        return carry

    lax.fori_loop(0, chunks, finish_chunk, 0)


def pick_kernel(place_ref, window_ref, out_ref):
    rows = window_ref.shape[1]
    shift, count = place_ref[0], place_ref[1]
    slot = lax.broadcasted_iota(jnp.int32, window_ref.shape[1:], 0)
    back = lax.rem(rows - shift, rows)
    for b in range(window_ref.shape[0]):
        moved = pltpu.roll(window_ref[b], back, 0)
        out_ref[b] = jnp.where(slot < count, moved, 0.0)


def per_device(spectra, delays, owner_bounds):
    n = lax.axis_size("inp")
    me = lax.axis_index("inp")
    inputs, band_chans, row_len = spectra.shape
    sig = inputs * n
    local_chans = band_chans // n
    local_vis = local_chans // AVG
    all_vis = band_chans // AVG
    tiles = sig // TILE
    total_rows = tiles * (tiles + 1) // 2 * TILE
    block = total_rows // n
    margin = block // 3
    slot_rows = block + 2 * margin
    cc = min(8, local_chans)
    chunks = local_chans // cc

    channel = me * local_chans + jnp.arange(local_chans, dtype=jnp.int32)
    channel = channel.reshape(local_vis, 1, AVG)
    steps = delays[None, :, None] * channel % CH
    angle = steps.astype(jnp.float32) * (2.0 * math.pi / CH)
    cosine, sine = jnp.cos(angle), jnp.sin(angle)

    dma = lambda *shape: pltpu.SemaphoreType.DMA(shape)
    windows = pl.pallas_call(
        functools.partial(correlate_kernel, n, GROUP, block),
        out_shape=jax.ShapeDtypeStruct((all_vis, slot_rows, row_len), jnp.float32),
        in_specs=[
            pl.BlockSpec(memory_space=pl.ANY),
            pl.BlockSpec(memory_space=pltpu.VMEM),
            pl.BlockSpec(memory_space=pltpu.VMEM),
        ],
        out_specs=pl.BlockSpec(memory_space=pl.ANY),
        scratch_shapes=[
            pltpu.VMEM((chunks, 2, sig, cc, row_len // 2), jnp.float32),
            pltpu.VMEM((tiles, 2 * TILE, AVG * row_len), jnp.bfloat16),
            pltpu.VMEM((tiles, 2 * TILE, AVG * row_len), jnp.bfloat16),
            pltpu.VMEM((local_vis, total_rows, row_len), jnp.float32),
            dma(chunks, 2, n),
            dma(chunks, 2, n),
        ]
        + [dma(local_vis, n)] * 8,
        compiler_params=pltpu.CompilerParams(
            collective_id=0, has_side_effects=True, vmem_limit_bytes=60 * 1024 * 1024
        ),
    )(spectra.reshape(inputs, band_chans // cc, cc, row_len), cosine, sine)

    first = lax.dynamic_index_in_dim(owner_bounds, me, keepdims=False)
    end = lax.dynamic_index_in_dim(owner_bounds, me + 1, keepdims=False)
    place = jnp.stack([first - (me * block - margin), end - first])
    step = 2
    spec = pl.BlockSpec((step, slot_rows, row_len), lambda i, place: (i, 0, 0))
    return pl.pallas_call(
        pick_kernel,
        out_shape=jax.ShapeDtypeStruct((all_vis, slot_rows, row_len), jnp.float32),
        grid_spec=pltpu.PrefetchScalarGridSpec(
            num_scalar_prefetch=1, grid=(all_vis // step,), in_specs=[spec], out_specs=spec
        ),
        compiler_params=pltpu.CompilerParams(vmem_limit_bytes=32 * 1024 * 1024),
    )(place, windows)


def solution(mesh):
    placed = (P("inp", "band", None), P(), P())
    return jax.shard_map(
        per_device, mesh=mesh, in_specs=placed, out_specs=P("band", "inp", None), check_vma=False
    )
```

time: 1500 us -> 942 us (0.63); the launches traced: 1480 us -> 941 us
  Pallas kernels: 0 us -> 928 us
  blocking collectives: 680 us -> 0 us
  waiting for transfers between devices: 359 us -> 0 us
  local copies, waits for them, and re-layouts: 238 us -> 1.98 us
  matrix products: 120 us -> 0 us
  other arithmetic: 78 us -> 9.16 us
    pallas_call x0 -> x2, Pallas kernels: none -> 928 us  [the longest x1 893 us: per_device(): pl.pallas_call(functools.partial(correlate_kernel, n, GROUP, block), out_...]
    all_to_all x1 -> x0, blocking collectives: 680 us -> none  [per_device(): lax.all_to_all(outgoing, 'inp', split_axis=1, concat_axis=0, tiled=True)]
    all_to_all x1 -> x0, waiting for transfers between devices: 359 us -> none  [per_device(): lax.all_to_all(spectra, 'inp', split_axis=1, concat_axis=0, tiled=True)]
    dot_general x8 -> x0, matrix products: 120 us -> none  [cross_product(): lax.dot_general(left_side, right_side, (((1,), (1,)), ((), ())), precisio...]
    slice x17 -> x0, local copies, waits for them, and re-layouts: 77.8 us -> none  [the longest x1 70.8 us: per_device(): swap_all = swapped[:, vis_index]]
    all_to_all x3 -> x0, local copies, waits for them, and re-layouts: 42.3 us -> none  [the longest x2 27.1 us: per_device(): lax.all_to_all(outgoing, 'inp', split_axis=1, concat_axis=0, tiled=True)]
    select_n x2 -> x0, other arithmetic: 41 us -> none  [the longest x1 40.9 us: per_device(): jnp.where(is_live.reshape(-1)[None, :, None], picked, jnp.zeros_like(pick...]
    reshape x2 -> x0, local copies, waits for them, and re-layouts: 40.8 us -> none  [the longest x1 20.4 us: correct(): jnp.concatenate([fixed_im, -fixed_re], axis=2)]
  transfers between devices with their start and end apart: 1 -> 0, of which waited for: 1 -> 0; matrix products, arithmetic and copies ran while one was open for 0% -> 0% of each run, Pallas kernels for 0% -> 0%
where the time goes in v1:
time: 942 us; the launch traced here: 941 us
  Pallas kernels  928 us (99%)
    pallas_call x1, Pallas kernels, per_device(): pl.pallas_call(functools.partial(correlate_kernel, n, GROUP, block), out_...  893 us
    pallas_call x1, Pallas kernels, per_device(): pl.pallas_call(pick_kernel, out_shape=jax.ShapeDtypeStruct((all_vis, slot...  34.7 us

profile of v1, /device:TPU:24, one launch (start us, length us, event | category | flops | bytes accessed | tf_op | source)
XLA Modules:
  0.0 940.8 jit_solution(18196305732176046658)
XLA Ops:
  0.0 1.3 fusion.2
  3.3 0.1 pad_add_fusion.place_ref
  3.4 0.8 fusion
  4.2 0.6 copy.4
  4.8 8.3 multiply_sine_fusion
  13.1 893.0 %shard_map.37.window_ref = f32[32,960,256]{2,1,0:T(8,128)} custom-call(f32[128,16,8,256]{3,2,1,0:T(8,128)} %bitcast.5, f32[4,1024,4]{2,1,0:T(8,128)} %get-tuple-element.6.cos_ref, f32[4,1024,4]{2,1,0:T(8,128)} %get-tuple-element.5.sin_ref), custom_call_target="tpu_custom_call" | custom-call | tf_op jit(solution)/shard_map/pallas_call | solution.py:410
  906.1 34.7 %shard_map.38 = f32[32,960,256]{2,1,0:T(8,128)} custom-call(s32[2]{0:T(128)S(1)} %pad_add_fusion.place_ref, f32[32,960,256]{2,1,0:T(8,128)} %shard_map.37.window_ref), custom_call_target="tpu_custom_call" | custom-call | tf_op jit(solution)/shard_map/pallas_call | solution.py:438
  (1 shorter events, 0.0 us)

commit v2 on v1

--- a/solution.py
+++ b/solution.py
@@ -11,13 +11,11 @@
 CH = 128
 AVG = 4
 TILE = 128
-GROUP = 2
 MESH = pl.DeviceIdType.MESH
 
 
 def correlate_kernel(
     n,
-    group,
     block,
     spectra_ref,
     cos_ref,
@@ -94,7 +92,7 @@
     def start_chunk(chunk, carry):
         def start_one(d, inner):
             for half in range(2):
-                spectra_to(chunk, half, lax.rem(me + d, n)).start()
+                spectra_to(chunk, half, lax.rem(me + 3 * d, n)).start()
             return inner
 
         lax.fori_loop(1, n, start_one, 0)
@@ -110,11 +108,16 @@
         (margin + block, margin, high_send, high_recv),
     )
 
-    def has_piece(index, target):
+    half_axis = n // 2
+
+    def same_half(source, target):
+        return source // half_axis == target // half_axis
+
+    def has_piece(index, source, target):
         if index == 1:
-            return (target % group == 0) & (target > 0)
+            return (target > 0) & (same_half(source, target) | (target == half_axis))
         if index == 2:
-            return (target % group == group - 1) & (target < n - 1)
+            return (target < n - 1) & (same_half(source, target) | (target == half_axis - 1))
         return None
 
     def guarded(condition, body):
@@ -219,39 +222,17 @@
 
     def start_rows(vis):
         def start_one(d, carry):
-            target = lax.rem(me + d, n)
+            target = lax.rem(me + 3 * d, n)
             for index in range(3):
                 guarded(
-                    has_piece(index, target),
+                    has_piece(index, me, target),
                     lambda index=index: remote_piece(vis, target, index).start(),
                 )
             return carry
 
         lax.fori_loop(1, n, start_one, 0)
         for index in range(3):
-            guarded(has_piece(index, me), lambda index=index: own_piece(vis, index).start())
-
-    def run_chunk(chunk, carry):
-        def arrived(d, inner):
-            for half in range(2):
-                spectra_from(chunk, half, lax.rem(me + n - d, n)).wait_recv()
-            return inner
-
-        lax.fori_loop(1, n, arrived, 0)
-        for half in range(2):
-            spectra_own(chunk, half).wait()
-
-        def run_vis(inner_vis, inner):
-            vis = chunk * per_chunk + inner_vis
-            stage(vis, chunk, inner_vis)
-            multiply(vis)
-            start_rows(vis)
-            return inner
-
-        lax.fori_loop(0, per_chunk, run_vis, 0)
-        return carry
-
-    lax.fori_loop(0, chunks, run_chunk, 0)
+            guarded(has_piece(index, me, me), lambda index=index: own_piece(vis, index).start())
 
     def relay_up(vis, source):
         row = source * local_vis + vis
@@ -275,47 +256,75 @@
             device_id_type=MESH,
         )
 
-    goes_up = me % group != group - 1
-    goes_down = me % group != 0
+    goes_up = me % half_axis != half_axis - 1
+    goes_down = me % half_axis != 0
 
     def relay_vis(vis, carry):
         def relay_source(d, inner):
-            source = lax.rem(me + n - d, n)
-
-            @pl.when(d == 0)
-            def _():
-                own_piece(vis, 0).wait()
-
-            @pl.when(d > 0)
+            source = lax.rem(me + (n - 3) * d, n)
+            far = jnp.logical_not(same_half(source, me))
+
+            @pl.when(far)
             def _():
                 arrived_piece(vis, source, 0).wait_recv()
 
-            if group > 1:
-
-                @pl.when(goes_up)
-                def _():
-                    relay_up(vis, source).start()
-
-                @pl.when(goes_down)
-                def _():
-                    relay_down(vis, source).start()
-
-            return inner
-
-        lax.fori_loop(0, n, relay_source, 0)
-        return carry
-
-    lax.fori_loop(0, local_vis, relay_vis, 0)
+            @pl.when(far & goes_up)
+            def _():
+                relay_up(vis, source).start()
+
+            @pl.when(far & goes_down)
+            def _():
+                relay_down(vis, source).start()
+
+            return inner
+
+        lax.fori_loop(1, n, relay_source, 0)
+        return carry
+
+    lag = max(1, local_vis - 1)
+
+    def run_chunk(chunk, carry):
+        def arrived(d, inner):
+            for half in range(2):
+                spectra_from(chunk, half, lax.rem(me + (n - 3) * d, n)).wait_recv()
+            return inner
+
+        lax.fori_loop(1, n, arrived, 0)
+        for half in range(2):
+            spectra_own(chunk, half).wait()
+
+        def run_vis(inner_vis, inner):
+            vis = chunk * per_chunk + inner_vis
+            stage(vis, chunk, inner_vis)
+            multiply(vis)
+
+            @pl.when(vis >= lag)
+            def _():
+                relay_vis(vis - lag, 0)
+
+            start_rows(vis)
+            return inner
+
+        lax.fori_loop(0, per_chunk, run_vis, 0)
+        return carry
+
+    lax.fori_loop(0, chunks, run_chunk, 0)
+
+    lax.fori_loop(max(0, local_vis - lag), local_vis, relay_vis, 0)
 
     def finish_vis(vis, carry):
         def finish_one(d, inner):
             other = lax.rem(me + d, n)
             for index in range(3):
                 guarded(
-                    has_piece(index, other),
+                    has_piece(index, me, other),
                     lambda index=index: remote_piece(vis, other, index).wait_send(),
                 )
 
+            @pl.when(same_half(other, me))
+            def _():
+                arrived_piece(vis, other, 0).wait_recv()
+
             @pl.when(me > 0)
             def _():
                 arrived_piece(vis, other, 1).wait_recv()
@@ -328,36 +337,24 @@
 
         lax.fori_loop(1, n, finish_one, 0)
 
-        @pl.when(has_piece(1, me))
-        def _():
-            own_piece(vis, 1).wait()
-
-        @pl.when((me > 0) & jnp.logical_not(has_piece(1, me)))
-        def _():
-            arrived_piece(vis, me, 1).wait_recv()
-
-        @pl.when(has_piece(2, me))
-        def _():
-            own_piece(vis, 2).wait()
-
-        @pl.when((me < n - 1) & jnp.logical_not(has_piece(2, me)))
-        def _():
-            arrived_piece(vis, me, 2).wait_recv()
-
-        if group > 1:
-
-            def finish_relay(source, inner):
-                @pl.when(goes_up)
-                def _():
-                    relay_up(vis, source).wait_send()
-
-                @pl.when(goes_down)
-                def _():
-                    relay_down(vis, source).wait_send()
-
-                return inner
-
-            lax.fori_loop(0, n, finish_relay, 0)
+        for index in range(3):
+            guarded(has_piece(index, me, me), lambda index=index: own_piece(vis, index).wait())
+
+        def finish_relay(d, inner):
+            source = lax.rem(me + d, n)
+            far = jnp.logical_not(same_half(source, me))
+
+            @pl.when(far & goes_up)
+            def _():
+                relay_up(vis, source).wait_send()
+
+            @pl.when(far & goes_down)
+            def _():
+                relay_down(vis, source).wait_send()
+
+            return inner
+
+        lax.fori_loop(1, n, finish_relay, 0)
         return carry
 
     lax.fori_loop(0, local_vis, finish_vis, 0)
@@ -401,14 +398,14 @@
     chunks = local_chans // cc
 
     channel = me * local_chans + jnp.arange(local_chans, dtype=jnp.int32)
-    channel = channel.reshape(local_vis, 1, AVG)
-    steps = delays[None, :, None] * channel % CH
+    steps = channel[:, None] * delays[None, :] % CH
     angle = steps.astype(jnp.float32) * (2.0 * math.pi / CH)
-    cosine, sine = jnp.cos(angle), jnp.sin(angle)
+    tables = lax.optimization_barrier((jnp.cos(angle), jnp.sin(angle)))
+    cosine, sine = (t.reshape(local_vis, AVG, sig).transpose(0, 2, 1) for t in tables)
 
     dma = lambda *shape: pltpu.SemaphoreType.DMA(shape)
     windows = pl.pallas_call(
-        functools.partial(correlate_kernel, n, GROUP, block),
+        functools.partial(correlate_kernel, n, block),
         out_shape=jax.ShapeDtypeStruct((all_vis, slot_rows, row_len), jnp.float32),
         in_specs=[
             pl.BlockSpec(memory_space=pl.ANY),

time: 942 us -> 883 us (0.937)
  Pallas kernels: 928 us -> 871 us
    pallas_call x1, Pallas kernels: 893 us -> 836 us  [per_device(): pl.pallas_call(functools.partial(correlate_kernel, n, block), out_shape=j...]
where the time goes in v2:
time: 883 us; the launch traced here: 879 us
  Pallas kernels  871 us (99%)
    pallas_call x1, Pallas kernels, per_device(): pl.pallas_call(functools.partial(correlate_kernel, n, block), out_shape=j...  836 us
    pallas_call x1, Pallas kernels, per_device(): pl.pallas_call(pick_kernel, out_shape=jax.ShapeDtypeStruct((all_vis, slot...  34.7 us

profile of v2, /device:TPU:24, one launch (start us, length us, event | category | flops | bytes accessed | tf_op | source)
XLA Modules:
  0.0 879.4 jit_solution(18052023472650808500)
XLA Ops:
  0.0 1.3 fusion.5
  3.3 0.1 pad_add_fusion.place_ref
  3.4 1.0 fusion.3
  4.4 2.0 copy.5
  6.4 2.0 copy.4
  8.4 836.4 %shard_map.37.window_ref = f32[32,960,256]{2,1,0:T(8,128)} custom-call(f32[128,16,8,256]{3,2,1,0:T(8,128)} %bitcast.7, f32[4,1024,4]{2,1,0:T(8,128)} %bitcast.9, f32[4,1024,4]{2,1,0:T(8,128)} %bitcast.8), custom_call_target="tpu_custom_call" | custom-call | tf_op jit(solution)/shard_map/pallas_call | solution.py:407
  844.8 34.7 %shard_map.38 = f32[32,960,256]{2,1,0:T(8,128)} custom-call(s32[2]{0:T(128)S(1)} %pad_add_fusion.place_ref, f32[32,960,256]{2,1,0:T(8,128)} %shard_map.37.window_ref), custom_call_target="tpu_custom_call" | custom-call | tf_op jit(solution)/shard_map/pallas_call | solution.py:435
  (3 shorter events, 0.1 us)
